TPU v7x, 32 devices: a whole 2x2x4 slice. The times are simulated.
32 devices in a mesh: row: 8 (over z, x), col: 4 (over y, core).
Axes of the slice: x: 2, y: 2, z: 4, core: 2. Of those that a mesh axis runs over, the one named last changes fastest.
Arguments:
- points: float32 [2, 2048], P(None, 'row'), may hold values from 0 to 1, as said below
- strip_ids: int32 [2048], P('row'), may hold values from 0 to 3, as said below
- counts: int32 [8], P('row'), may hold values from 128 to 256, as said below
- mode_index: int32 [1024], P('col'), may hold values from 0 to 32767, as said below
- reflectors: float32 [2048, 512], P('row'), may hold values from -0.125 to 0.125
Outputs:
- block_out: float32 [2048, 2048], P('row', 'col')
- upper_out: float32 [128, 2048], P(None, 'col')
Inputs may be any that keep to these rules, and one draw needn't show every extreme that they name: `counts`: an owner's live slots come first among its 256 slots; some owner has all 256 live. `mode_index`: the modes are distinct. `points`: every point lies in the triangle x >= 0, y >= 0, x + y <= 1. `strip_ids`: A slot of owner o has strip o * 4 // 8 or one more, at most 3.
All inputs are finite; a program needn't handle non-finite values.
Results may differ from a plain program's by a relative error of at most 0.0003.
Values sent between devices are 32-bit elements; how exact they have to be, the bound alone decides.
A program may use at most 64 MiB of HBM per device.

v0:
```python
import jax
import jax.numpy as jnp
from jax import lax
from jax.sharding import PartitionSpec as P

PANEL = 128
STRIPS = 4
PRECISE = lax.Precision.HIGHEST
SHIFT_RATE = 1e-06


def spread(array, axis, root):
    mine = lax.axis_index(axis) == root
    return lax.psum(jnp.where(mine, array, jnp.zeros_like(array)), axis)


def product(left, right):
    return jnp.dot(left, right, precision=PRECISE, preferred_element_type=jnp.float32)


def transposed_product(left, right):
    return lax.dot_general(
        left, right, (((0,), (0,)), ((), ())), precision=PRECISE, preferred_element_type=jnp.float32
    )


def cholesky_lower(gram):
    order_ids = jnp.arange(gram.shape[0], dtype=jnp.int32)

    def column_step(column, lower):
        row_now = lax.dynamic_index_in_dim(lower, column, 0, keepdims=False)
        target = lax.dynamic_index_in_dim(gram, column, 1, keepdims=False) - product(lower, row_now)
        pivot = jnp.sqrt(lax.dynamic_index_in_dim(target, column, 0, keepdims=False))
        new_column = jnp.where(order_ids >= column, target / pivot, jnp.zeros_like(target))
        return lax.dynamic_update_slice_in_dim(lower, new_column[:, None], column, 1)

    return lax.fori_loop(0, gram.shape[0], column_step, jnp.zeros_like(gram))


def lower_inverse(lower):
    order_ids = jnp.arange(lower.shape[0], dtype=jnp.int32)

    def row_step(row, inverse):
        row_now = lax.dynamic_index_in_dim(lower, row, 0, keepdims=False)
        unit_row = (order_ids == row).astype(lower.dtype)
        pivot = lax.dynamic_index_in_dim(row_now, row, 0, keepdims=False)
        new_row = (unit_row - product(row_now, inverse)) / pivot
        return lax.dynamic_update_slice_in_dim(inverse, new_row[None, :], row, 0)

    return lax.fori_loop(0, lower.shape[0], row_step, jnp.zeros_like(lower))


def assemble(points, strip_ids, live_mask, mode_index):
    freq_x = (mode_index // 128 - 128).astype(jnp.float32)
    freq_y = (mode_index % 128 + 1).astype(jnp.float32)
    phases = jnp.pi * (points[0][:, None] * freq_x[None, :] + points[1][:, None] * freq_y[None, :])
    weight = 3.0 * jnp.power(10.0, -strip_ids.astype(jnp.float32) / (STRIPS - 1)) * live_mask
    columns_all = jnp.stack([jnp.cos(phases), jnp.sin(phases)], axis=-1).reshape(
        phases.shape[0], -1
    )
    return columns_all * weight[:, None]


def reflect(gram_block, coeffs):
    upper_factor = jnp.triu(gram_block, 1) + 0.5 * jnp.diag(jnp.diagonal(gram_block))
    return product(lower_inverse(upper_factor.T), coeffs)


def orthonormalize(panel_cols):
    gram_one = lax.psum(transposed_product(panel_cols, panel_cols), "row")
    shift_size = SHIFT_RATE * jnp.trace(gram_one)
    lower_one = cholesky_lower(gram_one + shift_size * jnp.eye(PANEL, dtype=jnp.float32))
    basis_one = product(panel_cols, lower_inverse(lower_one).T)
    gram_two = lax.psum(transposed_product(basis_one, basis_one), "row")
    lower_two = cholesky_lower(gram_two)
    basis_cols = product(basis_one, lower_inverse(lower_two).T)
    return (basis_cols, lower_one.T)


def on_device(points, strip_ids, counts, mode_index, reflectors):
    row_count = points.shape[1]
    live_mask = (jnp.arange(row_count, dtype=jnp.int32) < counts[0]).astype(jnp.float32)
    work_block = assemble(points, strip_ids, live_mask, mode_index)
    stored = reflectors * live_mask[:, None]
    panels = stored.shape[1] // PANEL
    shaped = stored.reshape(row_count, panels, PANEL)
    gram_blocks = jnp.einsum(
        "rkp,rkq->kpq", shaped, shaped, precision=PRECISE, preferred_element_type=jnp.float32
    )
    gram_blocks = lax.psum(gram_blocks, "row")

    def apply_panel(panel_step, current):
        columns = lax.dynamic_slice_in_dim(stored, panel_step * PANEL, PANEL, 1)
        coeffs = lax.psum(transposed_product(columns, current), "row")
        gram_block = lax.dynamic_index_in_dim(gram_blocks, panel_step, 0, keepdims=False)
        return current - product(columns, reflect(gram_block, coeffs))

    work_block = lax.fori_loop(0, panels, apply_panel, work_block)
    basis_cols, factor = orthonormalize(work_block[:, :PANEL])
    basis_cols = spread(basis_cols, "col", 0)
    tail_rows = lax.psum(transposed_product(basis_cols, work_block), "row")
    remainder = work_block - product(basis_cols, tail_rows)
    col_count = work_block.shape[1]
    global_col = lax.axis_index("col") * col_count + jnp.arange(col_count, dtype=jnp.int32)
    is_panel = (global_col < PANEL)[None, :]
    norm_scale = jnp.sqrt(jnp.float32(row_count * lax.axis_size("row")))
    padded_basis = jnp.pad(basis_cols, ((0, 0), (0, col_count - PANEL)))
    padded_factor = jnp.pad(factor, ((0, 0), (0, col_count - PANEL)))
    block_out = jnp.where(is_panel, padded_basis * norm_scale, remainder)
    upper_out = jnp.where(is_panel, padded_factor, tail_rows) / norm_scale
    return (block_out, upper_out)


def solution(mesh):
    return jax.shard_map(
        on_device,
        mesh=mesh,
        in_specs=(P(None, "row"), P("row"), P("row"), P("col"), P("row", None)),
        out_specs=(P("row", "col"), P(None, "col")),
        check_vma=False,
    )
```

profile of v0, /device:TPU:0, one launch (start us, length us, event | category | flops | bytes accessed | tf_op | source)
XLA Modules:
  0.0 2036.4 jit_solution(15213815674457690325)
XLA Ops:
  7.9 3.0 fusion.44
  12.3 1.1 fusion.48
  15.9 69.3 %all-reduce.9.cloned.1.call-done = f32[4,128,128]{2,1,0:T(8,128)} async-done(((f32[4,128,128]{2,1,0:T(8,128)}), f32[4,128,128]{2,1,0:T(8,128)}) %all-reduce.9.cloned.1.call-update) | async-done | bytes 262160 | tf_op jit(solution)/shard_map/psum | solution.py:90
  85.2 805.3 %while.115 = (s32[]{:T(128)}, f32[256,512]{1,0:T(8,128)S(1)}, f32[256,512]{1,0:T(8,128)S(1)}, f32[4,128,128]{2,1,0:T(8,128)}, s32[]{:T(128)}, /*index=5*/s32[]{:...) while((s32[]{:T(128)}, f32[256,512]{1,0:T(8,128)S(1)}, ...), condition=%wide.region_5.6_spmd, body=%wide.region_1.5_spmd.sunk | while | flops 503809024 | bytes 5053304 | solution.py:98
  85.3 1.2 fusion.112
  87.4 1.3 gather_fusion
  88.7 195.8 %while.120 = (s32[]{:T(128)}, f32[128,128]{1,0:T(8,128)S(1)}, f32[128,128]{1,0:T(8,128)S(1)}, s32[]{:T(128)}, s32[]{:T(128)}, /*index=5*/s32[]{:T(128)}) while((s32[]{:T(128)}, f32[128,128]{1,0:T(8,128)S(1)}, f32[128,128]{1,0:T(8,128)S(1)}, s32[]{:T(128)}, s32[]{:T(128)}, /*index=5*/s32[]{:T(128)}) %tuple.222), condition=%wide.region_3.3_spmd.clone, body=%wide.region_2.2_spmd.clone.sunk | while | flops 197123 | bytes 69221 | solution.py:50
  284.5 1.3 fusion.113
  286.6 1.2 fusion.112
  288.7 1.3 gather_fusion
  290.1 195.8 %while.120 = (s32[]{:T(128)}, f32[128,128]{1,0:T(8,128)S(1)}, f32[128,128]{1,0:T(8,128)S(1)}, s32[]{:T(128)}, s32[]{:T(128)}, /*index=5*/s32[]{:T(128)}) while((s32[]{:T(128)}, f32[128,128]{1,0:T(8,128)S(1)}, f32[128,128]{1,0:T(8,128)S(1)}, s32[]{:T(128)}, s32[]{:T(128)}, /*index=5*/s32[]{:T(128)}) %tuple.222), condition=%wide.region_3.3_spmd.clone, body=%wide.region_2.2_spmd.clone.sunk | while | flops 197123 | bytes 69221 | solution.py:50
  485.9 1.3 fusion.113
  487.9 1.2 fusion.112
  490.1 1.3 gather_fusion
  491.4 195.8 %while.120 = (s32[]{:T(128)}, f32[128,128]{1,0:T(8,128)S(1)}, f32[128,128]{1,0:T(8,128)S(1)}, s32[]{:T(128)}, s32[]{:T(128)}, /*index=5*/s32[]{:T(128)}) while((s32[]{:T(128)}, f32[128,128]{1,0:T(8,128)S(1)}, f32[128,128]{1,0:T(8,128)S(1)}, s32[]{:T(128)}, s32[]{:T(128)}, /*index=5*/s32[]{:T(128)}) %tuple.222), condition=%wide.region_3.3_spmd.clone, body=%wide.region_2.2_spmd.clone.sunk | while | flops 197123 | bytes 69221 | solution.py:50
  687.2 1.3 fusion.113
  689.3 1.2 fusion.112
  691.4 1.3 gather_fusion
  692.8 195.8 %while.120 = (s32[]{:T(128)}, f32[128,128]{1,0:T(8,128)S(1)}, f32[128,128]{1,0:T(8,128)S(1)}, s32[]{:T(128)}, s32[]{:T(128)}, /*index=5*/s32[]{:T(128)}) while((s32[]{:T(128)}, f32[128,128]{1,0:T(8,128)S(1)}, f32[128,128]{1,0:T(8,128)S(1)}, s32[]{:T(128)}, s32[]{:T(128)}, /*index=5*/s32[]{:T(128)}) %tuple.222), condition=%wide.region_3.3_spmd.clone, body=%wide.region_2.2_spmd.clone.sunk | while | flops 197123 | bytes 69221 | solution.py:50
  888.6 1.3 fusion.113
  890.6 1.0 fusion.51
  891.7 71.6 %all-reduce.11.cloned.1.call-done = f32[128,128]{1,0:T(8,128)} async-done(((f32[128,128]{1,0:T(8,128)}), f32[128,128]{1,0:T(8,128)}) %all-reduce.11.cloned.1.call-update) | async-done | bytes 65552 | tf_op jit(solution)/shard_map/psum | solution.py:70
  963.3 1.5 select_reduce_fusion
  965.6 257.4 %while.116 = (s32[]{:T(128)}, f32[128,128]{1,0:T(8,128)S(1)}, f32[128,128]{0,1:T(8,128)S(1)}, s32[]{:T(128)}, s32[]{:T(128)}) while((s32[]{:T(128)}, f32[128,128]{1,0:T(8,128)S(1)}, f32[128,128]{0,1:T(8,128)S(1)}, s32[]{:T(128)}, s32[]{:T(128)}) %tuple.228), condition=%wide.region_9.10_spmd.clone, body=%wide.region_8.9_spmd.clone.sunk | while | flops 197122 | bytes 71261 | solution.py:37
  1223.0 184.3 %while.117 = (s32[]{:T(128)}, f32[128,128]{1,0:T(8,128)S(1)}, f32[128,128]{1,0:T(8,128)S(1)}, s32[]{:T(128)}, s32[]{:T(128)}, /*index=5*/s32[]{:T(128)}) while((s32[]{:T(128)}, f32[128,128]{1,0:T(8,128)S(1)}, f32[128,128]{1,0:T(8,128)S(1)}, s32[]{:T(128)}, s32[]{:T(128)}, /*index=5*/s32[]{:T(128)}) %tuple.231), condition=%wide.region_11.12_spmd.clone, body=%wide.region_10.11_spmd.clone.sunk | while | flops 197123 | bytes 69221 | solution.py:50
  1408.7 68.5 %all-reduce.13.cloned.1.call-done = f32[128,128]{1,0:T(8,128)} async-done(((f32[128,128]{1,0:T(8,128)}), f32[128,128]{1,0:T(8,128)}) %all-reduce.13.cloned.1.call-update) | async-done | bytes 65552 | tf_op jit(solution)/shard_map/psum | solution.py:74
  1478.1 257.4 %while.118 = (s32[]{:T(128)}, f32[128,128]{1,0:T(8,128)S(1)}, f32[128,128]{0,1:T(8,128)S(1)}, s32[]{:T(128)}, s32[]{:T(128)}) while((s32[]{:T(128)}, f32[128,128]{1,0:T(8,128)S(1)}, f32[128,128]{0,1:T(8,128)S(1)}, s32[]{:T(128)}, s32[]{:T(128)}) %tuple.234), condition=%wide.region_14.15_spmd.clone, body=%wide.region_13.14_spmd.clone.sunk | while | flops 197122 | bytes 71261 | solution.py:37
  1735.5 184.3 %while.119 = (s32[]{:T(128)}, f32[128,128]{1,0:T(8,128)S(1)}, f32[128,128]{1,0:T(8,128)S(1)}, s32[]{:T(128)}, s32[]{:T(128)}, /*index=5*/s32[]{:T(128)}) while((s32[]{:T(128)}, f32[128,128]{1,0:T(8,128)S(1)}, f32[128,128]{1,0:T(8,128)S(1)}, s32[]{:T(128)}, s32[]{:T(128)}, /*index=5*/s32[]{:T(128)}) %tuple.237), condition=%wide.region_16.17_spmd.clone, body=%wide.region_15.16_spmd.clone.sunk | while | flops 197123 | bytes 69221 | solution.py:50
  1920.8 31.4 %all-reduce.15.cloned.1.call-done = f32[256,128]{1,0:T(8,128)} async-done(((f32[256,128]{1,0:T(8,128)}), f32[256,128]{1,0:T(8,128)}) %all-reduce.15.cloned.1.call-update) | async-done | bytes 131088 | tf_op jit(solution)/shard_map/psum | solution.py:14
  1952.2 2.1 fusion.59
  1954.4 72.3 %all-reduce.17.cloned.1.call-done = f32[128,512]{1,0:T(8,128)} async-done(((f32[128,512]{1,0:T(8,128)}), f32[128,512]{1,0:T(8,128)}) %all-reduce.17.cloned.1.call-update) | async-done | bytes 262160 | tf_op jit(solution)/shard_map/psum | solution.py:101
  2026.8 2.4 fusion.43
  (3667 shorter events, 1478.4 us)
Async XLA Ops:
  7.2 78.1 %all-reduce.9.cloned.1.call-start = ((), (), s32[]{:S(2)}) async-start(), calls=%async_computation | async-start | bytes 524288 | tf_op jit(solution)/shard_map/psum | solution.py:90
  10.9 0.7 copy-start.4
  11.6 0.7 copy-start.5
  14.0 0.7 copy-start.6
  14.8 1.0 copy-start
  85.2 199.3 %all-reduce.19.cloned.1.call-start = ((), (), s32[]{:S(2)}) async-start(), calls=%async_computation.5 | async-start | bytes 524288 | tf_op jit(solution)/shard_map/while/body/eval_jaxpr/psum | solution.py:94
  286.5 199.4 %all-reduce.19.cloned.1.call-start = ((), (), s32[]{:S(2)}) async-start(), calls=%async_computation.5 | async-start | bytes 524288 | tf_op jit(solution)/shard_map/while/body/eval_jaxpr/psum | solution.py:94
  487.9 199.4 %all-reduce.19.cloned.1.call-start = ((), (), s32[]{:S(2)}) async-start(), calls=%async_computation.5 | async-start | bytes 524288 | tf_op jit(solution)/shard_map/while/body/eval_jaxpr/psum | solution.py:94
  689.2 199.4 %all-reduce.19.cloned.1.call-start = ((), (), s32[]{:S(2)}) async-start(), calls=%async_computation.5 | async-start | bytes 524288 | tf_op jit(solution)/shard_map/while/body/eval_jaxpr/psum | solution.py:94
  890.6 72.7 %all-reduce.11.cloned.1.call-start = ((), (), s32[]{:S(2)}) async-start(), calls=%async_computation.1 | async-start | bytes 131072 | tf_op jit(solution)/shard_map/psum | solution.py:70
  891.7 585.5 %all-reduce.13.cloned.1.call-start = ((), (), s32[]{:S(2)}) async-start(), calls=%async_computation.2 | async-start | bytes 131072 | tf_op jit(solution)/shard_map/psum | solution.py:74
  963.3 2.2 copy-start.3
  1408.6 543.6 %all-reduce.15.cloned.1.call-start = ((), (), s32[]{:S(2)}) async-start(), calls=%async_computation.3 | async-start | bytes 262144 | tf_op jit(solution)/shard_map/psum | solution.py:14
  1920.8 106.0 %all-reduce.17.cloned.1.call-start = ((), (), s32[]{:S(2)}) async-start(), calls=%async_computation.4 | async-start | bytes 524288 | tf_op jit(solution)/shard_map/psum | solution.py:101
  1954.3 72.5 %copy-start.2 = (f32[256,128]{1,0:T(8,128)S(1)}, f32[256,128]{1,0:T(8,128)}, u32[]{:S(2)}) copy-start(f32[256,128]{1,0:T(8,128)} %all-reduce.15.cloned.1.call-done) | copy-start | bytes 393220
  2026.8 2.4 copy-start.1
Sparse Core Ops, SparseCore 0:
  11.9 73.2 all-reduce.8
  90.4 70.1 all-reduce.18
  291.7 70.0 all-reduce.18
  492.7 70.1 all-reduce.18
  694.1 70.1 all-reduce.18
  895.5 67.7 all-reduce.10
  1408.7 68.4 all-reduce.12
  1920.9 31.2 all-reduce.14
  1956.2 70.5 all-reduce.16
where the time goes:
time: 2060 us; the launch traced here: 2040 us
  local copies, waits for them, and re-layouts  805 us (39%)
  matrix products  693 us (34%)
  waiting for transfers between devices  313 us (15%)
  loops' own time  203 us (10%)
    dot_general x1035, matrix products, product(): jnp.dot(left, right, precision=PRECISE, preferred_element_type=jnp.float32)  682 us
    dynamic_slice x768, local copies, waits for them, and re-layouts, row_step(): pivot = lax.dynamic_index_in_dim(row_now, row, 0, keepdims=False)  484 us
    another operation x2, loops' own time, cholesky_lower(): return lax.fori_loop(0, gram.shape[0], column_step, jnp.zeros_like(gram))  185 us
    dynamic_slice x256, local copies, waits for them, and re-layouts, column_step(): lax.dynamic_index_in_dim(target, column, 0, keepdims=False)  163 us
    dynamic_update_slice x256, local copies, waits for them, and re-layouts, column_step(): lax.dynamic_update_slice_in_dim(lower, new_column[:, None], column, 1)  91.8 us
    psum x1, waiting for transfers between devices, on_device(): tail_rows = lax.psum(transposed_product(basis_cols, work_block), 'row')  72.3 us
    psum x1, waiting for transfers between devices, orthonormalize(): gram_one = lax.psum(transposed_product(panel_cols, panel_cols), 'row')  71.6 us
    psum x1, waiting for transfers between devices, on_device(): gram_blocks = lax.psum(gram_blocks, 'row')  69.3 us
  transfers between devices with their start and end apart: 9, of which 5 were waited for; matrix products, arithmetic and copies ran while one was open for 38% of the time, Pallas kernels for 0%

commit v1 on v0

--- a/solution.py
+++ b/solution.py
@@ -2,6 +2,7 @@
 import jax.numpy as jnp
 from jax import lax
 from jax.sharding import PartitionSpec as P
+from jax.lax import all_gather
 
 PANEL = 128
 STRIPS = 4
@@ -67,7 +68,8 @@
 
 
 def orthonormalize(panel_cols):
-    gram_one = lax.psum(transposed_product(panel_cols, panel_cols), "row")
+    v0 = transposed_product(panel_cols, panel_cols)
+    gram_one = jnp.sum(all_gather(v0, "row"), 0)
     shift_size = SHIFT_RATE * jnp.trace(gram_one)
     lower_one = cholesky_lower(gram_one + shift_size * jnp.eye(PANEL, dtype=jnp.float32))
     basis_one = product(panel_cols, lower_inverse(lower_one).T)

time: 2060 us -> 1970 us (0.956)
  waiting for transfers between devices: 313 us -> 241 us
  blocking collectives: 0 us -> 31.6 us
  matrix products: 693 us -> 671 us
    psum x1 -> x0, waiting for transfers between devices: 71.6 us -> none  [orthonormalize(): gram_one = lax.psum(transposed_product(panel_cols, panel_cols), 'row')]
    all_gather x0 -> x1, blocking collectives: none -> 31.6 us  [orthonormalize(): gram_one = jnp.sum(all_gather(v0, 'row'), 0)]
    dot_general x1035, matrix products: 682 us -> 659 us  [product(): jnp.dot(left, right, precision=PRECISE, preferred_element_type=jnp.float32)]
  transfers between devices with their start and end apart: 9 -> 8, of which waited for: 5 -> 4; matrix products, arithmetic and copies ran while one was open for 38% -> 38% of each run, Pallas kernels for 0% -> 0%
where the time goes in v1:
time: 1970 us; the launch traced here: 1960 us
  local copies, waits for them, and re-layouts  790 us (40%)
  matrix products  671 us (34%)
  waiting for transfers between devices  241 us (12%)
  loops' own time  203 us (10%)
  blocking collectives  31.6 us (2%)
    dot_general x1035, matrix products, product(): jnp.dot(left, right, precision=PRECISE, preferred_element_type=jnp.float32)  659 us
    dynamic_slice x768, local copies, waits for them, and re-layouts, row_step(): pivot = lax.dynamic_index_in_dim(row_now, row, 0, keepdims=False)  469 us
    another operation x2, loops' own time, cholesky_lower(): return lax.fori_loop(0, gram.shape[0], column_step, jnp.zeros_like(gram))  185 us
    dynamic_slice x256, local copies, waits for them, and re-layouts, column_step(): lax.dynamic_index_in_dim(target, column, 0, keepdims=False)  163 us
    dynamic_update_slice x256, local copies, waits for them, and re-layouts, column_step(): lax.dynamic_update_slice_in_dim(lower, new_column[:, None], column, 1)  91.8 us
    psum x1, waiting for transfers between devices, on_device(): tail_rows = lax.psum(transposed_product(basis_cols, work_block), 'row')  72.3 us
    psum x1, waiting for transfers between devices, on_device(): gram_blocks = lax.psum(gram_blocks, 'row')  69.3 us
    psum x1, waiting for transfers between devices, orthonormalize(): gram_two = lax.psum(transposed_product(basis_one, basis_one), 'row')  67.8 us
  transfers between devices with their start and end apart: 8, of which 4 were waited for; matrix products, arithmetic and copies ran while one was open for 38% of the time, Pallas kernels for 0%

profile of v1, /device:TPU:0, one launch (start us, length us, event | category | flops | bytes accessed | tf_op | source)
XLA Modules:
  0.0 1957.3 jit_solution(12882900682431447034)
XLA Ops:
  7.9 3.0 fusion.44
  12.3 1.1 fusion.48
  15.9 69.3 %all-reduce.8.cloned.1.call-done = f32[4,128,128]{2,1,0:T(8,128)} async-done(((f32[4,128,128]{2,1,0:T(8,128)}), f32[4,128,128]{2,1,0:T(8,128)}) %all-reduce.8.cloned.1.call-update) | async-done | bytes 262160 | tf_op jit(solution)/shard_map/psum | solution.py:92
  85.2 768.1 %while.115 = (s32[]{:T(128)}, f32[256,512]{1,0:T(8,128)S(1)}, f32[256,512]{1,0:T(8,128)S(1)}, f32[4,128,128]{2,1,0:T(8,128)}, s32[]{:T(128)}, /*index=5*/s32[]{:...) while((s32[]{:T(128)}, f32[256,512]{1,0:T(8,128)S(1)}, ...), condition=%wide.region_5.6_spmd, body=%wide.region_1.5_spmd.sunk | while | flops 503809024 | bytes 5053304 | solution.py:100
  85.3 1.2 fusion.112
  87.4 1.3 gather_fusion
  88.7 186.5 %while.120 = (s32[]{:T(128)}, f32[128,128]{1,0:T(8,128)S(1)}, f32[128,128]{1,0:T(8,128)S(1)}, s32[]{:T(128)}, s32[]{:T(128)}, /*index=5*/s32[]{:T(128)}) while((s32[]{:T(128)}, f32[128,128]{1,0:T(8,128)S(1)}, f32[128,128]{1,0:T(8,128)S(1)}, s32[]{:T(128)}, s32[]{:T(128)}, /*index=5*/s32[]{:T(128)}) %tuple.222), condition=%wide.region_3.3_spmd.clone, body=%wide.region_2.2_spmd.clone.sunk | while | flops 197123 | bytes 69221 | solution.py:51
  275.2 1.3 fusion.113
  277.3 1.2 fusion.112
  279.4 1.3 gather_fusion
  280.8 186.5 %while.120 = (s32[]{:T(128)}, f32[128,128]{1,0:T(8,128)S(1)}, f32[128,128]{1,0:T(8,128)S(1)}, s32[]{:T(128)}, s32[]{:T(128)}, /*index=5*/s32[]{:T(128)}) while((s32[]{:T(128)}, f32[128,128]{1,0:T(8,128)S(1)}, f32[128,128]{1,0:T(8,128)S(1)}, s32[]{:T(128)}, s32[]{:T(128)}, /*index=5*/s32[]{:T(128)}) %tuple.222), condition=%wide.region_3.3_spmd.clone, body=%wide.region_2.2_spmd.clone.sunk | while | flops 197123 | bytes 69221 | solution.py:51
  467.3 1.3 fusion.113
  469.3 1.2 fusion.112
  471.5 1.3 gather_fusion
  472.8 186.5 %while.120 = (s32[]{:T(128)}, f32[128,128]{1,0:T(8,128)S(1)}, f32[128,128]{1,0:T(8,128)S(1)}, s32[]{:T(128)}, s32[]{:T(128)}, /*index=5*/s32[]{:T(128)}) while((s32[]{:T(128)}, f32[128,128]{1,0:T(8,128)S(1)}, f32[128,128]{1,0:T(8,128)S(1)}, s32[]{:T(128)}, s32[]{:T(128)}, /*index=5*/s32[]{:T(128)}) %tuple.222), condition=%wide.region_3.3_spmd.clone, body=%wide.region_2.2_spmd.clone.sunk | while | flops 197123 | bytes 69221 | solution.py:51
  659.3 1.3 fusion.113
  661.4 1.2 fusion.112
  663.6 1.3 gather_fusion
  664.9 186.5 %while.120 = (s32[]{:T(128)}, f32[128,128]{1,0:T(8,128)S(1)}, f32[128,128]{1,0:T(8,128)S(1)}, s32[]{:T(128)}, s32[]{:T(128)}, /*index=5*/s32[]{:T(128)}) while((s32[]{:T(128)}, f32[128,128]{1,0:T(8,128)S(1)}, f32[128,128]{1,0:T(8,128)S(1)}, s32[]{:T(128)}, s32[]{:T(128)}, /*index=5*/s32[]{:T(128)}) %tuple.222), condition=%wide.region_3.3_spmd.clone, body=%wide.region_2.2_spmd.clone.sunk | while | flops 197123 | bytes 69221 | solution.py:51
  851.4 1.3 fusion.113
  853.8 31.6 %all-gather = f32[1024,128]{1,0:T(8,128)S(1)} all-gather(f32[128,128]{1,0:T(8,128)S(1)} %fusion.51), channel_id=2, replica_groups=mesh['row'=8,'col'=4] {'row'}, dimensions={0}, use_global_device_ids=true | all-gather | bytes 589824 | tf_op jit(solution)/shard_map/all_gather | solution.py:72
  886.9 257.4 %while.116 = (s32[]{:T(128)}, f32[128,128]{1,0:T(8,128)S(1)}, f32[128,128]{0,1:T(8,128)S(1)}, s32[]{:T(128)}, s32[]{:T(128)}) while((s32[]{:T(128)}, f32[128,128]{1,0:T(8,128)S(1)}, f32[128,128]{0,1:T(8,128)S(1)}, s32[]{:T(128)}, s32[]{:T(128)}) %tuple.228), condition=%wide.region_9.10_spmd.clone, body=%wide.region_8.9_spmd.clone.sunk | while | flops 197122 | bytes 71261 | solution.py:38
  1144.3 184.3 %while.117 = (s32[]{:T(128)}, f32[128,128]{1,0:T(8,128)S(1)}, f32[128,128]{1,0:T(8,128)S(1)}, s32[]{:T(128)}, s32[]{:T(128)}, /*index=5*/s32[]{:T(128)}) while((s32[]{:T(128)}, f32[128,128]{1,0:T(8,128)S(1)}, f32[128,128]{1,0:T(8,128)S(1)}, s32[]{:T(128)}, s32[]{:T(128)}, /*index=5*/s32[]{:T(128)}) %tuple.231), condition=%wide.region_11.12_spmd.clone, body=%wide.region_10.11_spmd.clone.sunk | while | flops 197123 | bytes 69221 | solution.py:51
  1328.9 1.0 fusion.58
  1330.0 67.8 %all-reduce.10.cloned.1.call-done = f32[128,128]{1,0:T(8,128)} async-done(((f32[128,128]{1,0:T(8,128)}), f32[128,128]{1,0:T(8,128)}) %all-reduce.10.cloned.1.call-update) | async-done | bytes 65552 | tf_op jit(solution)/shard_map/psum | solution.py:76
  1398.8 257.4 %while.118 = (s32[]{:T(128)}, f32[128,128]{1,0:T(8,128)S(1)}, f32[128,128]{0,1:T(8,128)S(1)}, s32[]{:T(128)}, s32[]{:T(128)}) while((s32[]{:T(128)}, f32[128,128]{1,0:T(8,128)S(1)}, f32[128,128]{0,1:T(8,128)S(1)}, s32[]{:T(128)}, s32[]{:T(128)}) %tuple.234), condition=%wide.region_14.15_spmd.clone, body=%wide.region_13.14_spmd.clone.sunk | while | flops 197122 | bytes 71261 | solution.py:38
  1656.2 184.3 %while.119 = (s32[]{:T(128)}, f32[128,128]{1,0:T(8,128)S(1)}, f32[128,128]{1,0:T(8,128)S(1)}, s32[]{:T(128)}, s32[]{:T(128)}, /*index=5*/s32[]{:T(128)}) while((s32[]{:T(128)}, f32[128,128]{1,0:T(8,128)S(1)}, f32[128,128]{1,0:T(8,128)S(1)}, s32[]{:T(128)}, s32[]{:T(128)}, /*index=5*/s32[]{:T(128)}) %tuple.237), condition=%wide.region_16.17_spmd.clone, body=%wide.region_15.16_spmd.clone.sunk | while | flops 197123 | bytes 69221 | solution.py:51
  1840.4 0.9 convolution_select_fusion
  1841.4 31.4 %all-reduce.12.cloned.1.call-done = f32[256,128]{1,0:T(8,128)} async-done(((f32[256,128]{1,0:T(8,128)}), f32[256,128]{1,0:T(8,128)}) %all-reduce.12.cloned.1.call-update) | async-done | bytes 131088 | tf_op jit(solution)/shard_map/psum | solution.py:15
  1872.8 2.1 fusion.59
  1875.1 72.3 %all-reduce.14.cloned.1.call-done = f32[128,512]{1,0:T(8,128)} async-done(((f32[128,512]{1,0:T(8,128)}), f32[128,512]{1,0:T(8,128)}) %all-reduce.14.cloned.1.call-update) | async-done | bytes 262160 | tf_op jit(solution)/shard_map/psum | solution.py:103
  1947.4 2.4 fusion.43
  (3664 shorter events, 1440.2 us)
Async XLA Ops:
  7.2 78.1 %all-reduce.8.cloned.1.call-start = ((), (), s32[]{:S(2)}) async-start(), calls=%async_computation | async-start | bytes 524288 | tf_op jit(solution)/shard_map/psum | solution.py:92
  10.9 0.7 copy-start.3
  11.6 0.7 copy-start.4
  14.0 0.7 copy-start.5
  14.8 1.0 copy-start
  85.2 190.0 %all-reduce.16.cloned.1.call-start = ((), (), s32[]{:S(2)}) async-start(), calls=%async_computation.4 | async-start | bytes 524288 | tf_op jit(solution)/shard_map/while/body/eval_jaxpr/psum | solution.py:96
  277.2 190.1 %all-reduce.16.cloned.1.call-start = ((), (), s32[]{:S(2)}) async-start(), calls=%async_computation.4 | async-start | bytes 524288 | tf_op jit(solution)/shard_map/while/body/eval_jaxpr/psum | solution.py:96
  469.3 190.1 %all-reduce.16.cloned.1.call-start = ((), (), s32[]{:S(2)}) async-start(), calls=%async_computation.4 | async-start | bytes 524288 | tf_op jit(solution)/shard_map/while/body/eval_jaxpr/psum | solution.py:96
  661.3 190.1 %all-reduce.16.cloned.1.call-start = ((), (), s32[]{:S(2)}) async-start(), calls=%async_computation.4 | async-start | bytes 524288 | tf_op jit(solution)/shard_map/while/body/eval_jaxpr/psum | solution.py:96
  853.4 544.4 %all-reduce.10.cloned.1.call-start = ((), (), s32[]{:S(2)}) async-start(), calls=%async_computation.1 | async-start | bytes 131072 | tf_op jit(solution)/shard_map/psum | solution.py:76
  1329.9 542.9 %all-reduce.12.cloned.1.call-start = ((), (), s32[]{:S(2)}) async-start(), calls=%async_computation.2 | async-start | bytes 262144 | tf_op jit(solution)/shard_map/psum | solution.py:15
  1841.4 106.0 %all-reduce.14.cloned.1.call-start = ((), (), s32[]{:S(2)}) async-start(), calls=%async_computation.3 | async-start | bytes 524288 | tf_op jit(solution)/shard_map/psum | solution.py:103
  1874.9 72.4 %copy-start.2 = (f32[256,128]{1,0:T(8,128)S(1)}, f32[256,128]{1,0:T(8,128)}, u32[]{:S(2)}) copy-start(f32[256,128]{1,0:T(8,128)} %all-reduce.12.cloned.1.call-done) | copy-start | bytes 393220
  1947.4 2.4 copy-start.1
Sparse Core Ops, SparseCore 0:
  11.9 73.2 all-reduce.7
  90.4 70.1 all-reduce.15
  282.4 70.1 all-reduce.15
  474.1 70.0 all-reduce.15
  666.2 70.0 all-reduce.15
  1330.0 67.7 all-reduce.9
  1841.5 31.2 all-reduce.11
  1876.8 70.5 all-reduce.13
